TPU v7x, 256 devices: a whole 4x4x8 slice. The times are simulated.
256 devices in a mesh: dp: 2 (over core), dom: 128 (over y, z, x).
Axes of the slice: x: 4, y: 4, z: 8, core: 2. Of those that a mesh axis runs over, the one named last changes fastest.
Arguments:
- features: bfloat16 [2, 49152, 512], P('dp', 'dom'), may hold values from -12 to 12
- tile_mask: int32 [2, 384, 18], P('dp', 'dom'), may hold values from 0 to 1, as said below
- cotangent: bfloat16 [2, 49152, 512], P('dp', 'dom'), may hold values from -6 to 6
- w_query: bfloat16 [512, 512], replicated, may hold values from -1 to 1
- w_key: bfloat16 [512, 512], replicated, may hold values from -1 to 1
- w_value: bfloat16 [512, 512], replicated, may hold values from -0.25 to 0.25
- w_out: bfloat16 [512, 512], replicated, may hold values from -0.25 to 0.25
Outputs:
- attended: bfloat16 [2, 49152, 512], P('dp', 'dom')
- grad_features: bfloat16 [2, 49152, 512], P('dp', 'dom')
- grad_query: float32 [512, 512], replicated
- grad_key: float32 [512, 512], replicated
- grad_value: float32 [512, 512], replicated
- grad_out: float32 [512, 512], replicated
Inputs may be any that keep to these rules, and one draw needn't show every extreme that they name: `tile_mask`: 0 or 1; the share of ones differs between tile groups, from about a quarter to all.
All inputs are finite; a program needn't handle non-finite values.
Results may differ from a plain program's by a relative error of at most 0.023.
Values may be sent and summed in bfloat16 or wider, within the bound.
A program may use at most 128 MiB of HBM per device.

v0:
```python
import jax
import jax.numpy as jnp
from jax import lax
from jax.sharding import PartitionSpec as P

HEADS = 8
HEAD_DIM = 64
TILE = 128
TILE_DEV = 3
NB = 3
CANDT = 18


def with_halo(block, sides, width):
    for axis, dim in sides:
        count = lax.axis_size(axis)
        forward = [(i, i + 1) for i in range(count - 1)]
        forward.append((count - 1, 0))
        backward = [(target, source) for source, target in forward]
        low = lax.ppermute(
            lax.slice_in_dim(block, block.shape[dim] - width, None, axis=dim), axis, forward
        )
        high = lax.ppermute(lax.slice_in_dim(block, 0, width, axis=dim), axis, backward)
        block = jnp.concatenate([low, block, high], axis=dim)
    return block


def from_partner(value, axis, distance):
    mask = 2**distance
    pairs = [(source, source ^ mask) for source in range(lax.axis_size(axis))]
    return lax.ppermute(value, axis, pairs)


def candidate_blocks(block):
    block_rows = block.shape[0]
    near = with_halo(block, (("dom", 0),), block_rows)
    pieces = [block, near[:block_rows], near[2 * block_rows :]]
    levels = lax.axis_size("dom").bit_length() - 1
    for bit_step in range(NB):
        pieces.append(from_partner(block, "dom", levels - 1 - bit_step))
    return pieces


def returned_sum(grad_parts):
    block_rows = grad_parts.shape[1]
    outgoing = jnp.concatenate([grad_parts[1], grad_parts[2]], 0)
    returned = with_halo(outgoing, (("dom", 0),), block_rows)
    summed = grad_parts[0] + returned[:block_rows] + returned[3 * block_rows :]
    levels = lax.axis_size("dom").bit_length() - 1
    for bit_step in range(NB):
        summed = summed + from_partner(grad_parts[3 + bit_step], "dom", levels - 1 - bit_step)
    return summed


def joined(stacked_parts, width_all):
    return jnp.transpose(stacked_parts, (1, 0, 2)).reshape(stacked_parts.shape[1], width_all)


def per_device(features, tile_mask, cotangent, w_query, w_key, w_value, w_out):
    node_rows = features[0]
    block_rows = node_rows.shape[0]
    width_all = node_rows.shape[1]
    highest = lax.Precision.HIGHEST
    factor = HEAD_DIM ** (-0.5)
    w_both = jnp.concatenate([w_key, w_value], 1)
    q_rows = jnp.dot(node_rows, w_query, preferred_element_type=jnp.float32).astype(jnp.bfloat16)
    kv_rows = jnp.dot(node_rows, w_both, preferred_element_type=jnp.float32).astype(jnp.bfloat16)
    cand_kv = jnp.concatenate(candidate_blocks(kv_rows), 0)
    key_count = cand_kv.shape[0]
    keys_all = cand_kv[:, :width_all]
    values_all = cand_kv[:, width_all:]
    own_tile = jnp.arange(CANDT)[None, :] == jnp.arange(TILE_DEV)[:, None]
    live_tiles = (tile_mask[0] == 1) | own_tile
    masking = jnp.where(live_tiles, 0.0, -1e30).astype(jnp.float32)
    cot_rows = cotangent[0]
    grad_o = jnp.dot(cot_rows, w_out.T, preferred_element_type=jnp.float32).astype(jnp.bfloat16)
    pair_cols = 2 * HEAD_DIM

    def head_pair(pair_index):
        col_start = pair_index * pair_cols
        q_pair = lax.dynamic_slice_in_dim(q_rows, col_start, pair_cols, 1).reshape(
            block_rows, 2, HEAD_DIM
        )
        k_pair = lax.dynamic_slice_in_dim(keys_all, col_start, pair_cols, 1).reshape(
            key_count, 2, HEAD_DIM
        )
        v_pair = lax.dynamic_slice_in_dim(values_all, col_start, pair_cols, 1).reshape(
            key_count, 2, HEAD_DIM
        )
        g_pair = lax.dynamic_slice_in_dim(grad_o, col_start, pair_cols, 1).reshape(
            block_rows, 2, HEAD_DIM
        )
        scores = (
            jnp.einsum("rhd,chd->hrc", q_pair, k_pair, preferred_element_type=jnp.float32) * factor
        )
        scores = scores.reshape(2, TILE_DEV, TILE, CANDT, TILE) + masking[None, :, None, :, None]
        scores = scores.reshape(2, block_rows, key_count)
        row_max = jnp.max(scores, axis=2, keepdims=True)
        exp_vals = jnp.exp(scores - row_max)
        prob_f32 = exp_vals / jnp.sum(exp_vals, axis=2, keepdims=True)
        prob_bf = prob_f32.astype(jnp.bfloat16)
        out_pair = jnp.einsum(
            "hrc,chd->rhd", prob_bf, v_pair, preferred_element_type=jnp.float32
        ).astype(jnp.bfloat16)
        grad_prob = jnp.einsum("rhd,chd->hrc", g_pair, v_pair, preferred_element_type=jnp.float32)
        row_delta = jnp.einsum(
            "rhd,rhd->hr", g_pair.astype(jnp.float32), out_pair.astype(jnp.float32)
        )
        grad_score = (prob_f32 * (grad_prob - row_delta[:, :, None]) * factor).astype(jnp.bfloat16)
        gq_pair = jnp.einsum(
            "hrc,chd->rhd", grad_score, k_pair, preferred_element_type=jnp.float32
        ).reshape(block_rows, pair_cols)
        gk_pair = jnp.einsum(
            "hrc,rhd->chd", grad_score, q_pair, preferred_element_type=jnp.float32
        ).reshape(key_count, pair_cols)
        gv_pair = jnp.einsum(
            "hrc,rhd->chd", prob_bf, g_pair, preferred_element_type=jnp.float32
        ).reshape(key_count, pair_cols)
        return (out_pair.reshape(block_rows, pair_cols), gq_pair, gk_pair, gv_pair)

    stacked = lax.map(head_pair, jnp.arange(HEADS // 2, dtype=jnp.int32))
    out_rows = joined(stacked[0], width_all)
    grad_q = joined(stacked[1], width_all)
    grad_k = joined(stacked[2], width_all)
    grad_v = joined(stacked[3], width_all)
    attended = jnp.dot(out_rows, w_out, preferred_element_type=jnp.float32).astype(jnp.bfloat16)
    grad_parts = jnp.concatenate([grad_k, grad_v], 1).reshape(3 + NB, block_rows, 2 * width_all)
    w_both32 = w_both.astype(jnp.float32)
    rows_f32 = node_rows.astype(jnp.float32)
    own_grad = returned_sum(grad_parts)
    kv_dx = jnp.dot(own_grad, w_both32.T, precision=highest)
    g_both = jnp.dot(rows_f32.T, own_grad, precision=highest)
    grad_x = jnp.dot(grad_q, w_query.astype(jnp.float32).T, precision=highest) + kv_dx
    g_query = jnp.dot(rows_f32.T, grad_q, precision=highest)
    g_out = jnp.dot(out_rows.T, cot_rows, preferred_element_type=jnp.float32)
    g_query, g_key, g_value, g_out = lax.psum(
        (g_query, g_both[:, :width_all], g_both[:, width_all:], g_out), ("dp", "dom")
    )
    return (attended[None], grad_x.astype(jnp.bfloat16)[None], g_query, g_key, g_value, g_out)


def solution(mesh):
    in_specs = (
        P("dp", "dom", None),
        P("dp", "dom", None),
        P("dp", "dom", None),
        P(),
        P(),
        P(),
        P(),
    )
    out_specs = (P("dp", "dom", None), P("dp", "dom", None), P(), P(), P(), P())
    return jax.shard_map(
        per_device, mesh=mesh, in_specs=in_specs, out_specs=out_specs, check_vma=False
    )
```

profile of v0, /device:TPU:8, one launch (start us, length us, event | category | flops | bytes accessed | tf_op | source)
XLA Modules:
  0.0 602.2 jit_solution(1646686012757670933)
XLA Ops:
  7.3 1.2 constant_dynamic-update-slice_fusion.5
  10.6 2.7 constant_dynamic-update-slice_fusion.11
  13.3 7.2 %collective-permute-start.4 = (bf16[384,1024]{1,0:T(8,128)(2,1)}, bf16[384,1024]{1,0:T(8,128)(2,1)S(1)}, u32[]{:S(2)}, u32[]{:S(2)}) collective-permute-start(bf16[384,1024]{1,0:T(8,128)(2,1)} %get-tuple-element.146), channel_id=1, source_target_pairs={{0,16},{1,17},{2,18},{3,19},{4,20},{5,21},{6,22},{7,23},{8,24},{9,... | collective-permute-start | bytes 2359304 | tf_op jit(solution)/shard_map/ppermute | solution.py:31
  21.0 2.6 collective-permute-start.2
  23.6 3.6 collective-permute-start.1
  28.1 45.5 %collective-permute-done = bf16[384,1024]{1,0:T(8,128)(2,1)} collective-permute-done((bf16[384,1024]{1,0:T(8,128)(2,1)}, bf16[384,1024]{1,0:T(8,128)(2,1)}, u32[]{:S(2)}, u32[]{:S(2)}) %collective-permute-start) | collective-permute-done | bytes 786464 | tf_op jit(solution)/shard_map/ppermute | solution.py:20
  73.5 2.1 constant_dynamic-update-slice_fusion.10
  75.7 2.1 constant_dynamic-update-slice_fusion.9
  77.8 2.1 constant_dynamic-update-slice_fusion.8
  79.8 2.1 constant_dynamic-update-slice_fusion.7
  82.8 4.8 fusion.33
  87.6 110.8 %while.16 = (s32[]{:T(128)}, bf16[4,384,128]{1,2,0:T(8,128)(2,1)}, f32[4,384,128]{1,2,0:T(8,128)}, f32[4,2304,128]{1,2,0:T(8,128)}, f32[4,2304,128]{1,2,0:T(8,12...) while((s32[]{:T(128)}, bf16[4,384,128]{1,2,0:T(8,128)(2,1)}, ...), condition=%wide.region_3.4_spmd, body=%wide.region_0.3_spmd.sunk | while | flops 1378665984 | bytes 104414744 | solution.py:121
  92.4 2.5 copy.50
  94.9 7.1 %fusion.93 = (f32[2,384]{1,0:T(2,128)S(1)}, f32[2,384,2304]{2,1,0:T(8,128)}) fusion(f32[384,2304]{1,0:T(8,128)} %bitcast.143, bf16[384,2,64]{0,2,1:T(8,128)(2,1)S(1)} %bitcast.150, bf16[2304,2,64]{0,2,1:T(8,128)(2,1)S(1)} %bitcast.144), kind=kOutput, calls=%fused_computation.74.clone.1 | convolution fusion | flops 233572608 | bytes 11308032 | tf_op jit(solution)/shard_map/while/body/eval_jaxpr/sub | solution.py:99
  102.0 3.8 fusion.94
  108.8 1.6 multiply_convert_fusion.2
  113.7 1.6 constant_dynamic-update-slice_fusion.17
  120.1 2.5 copy.50
  122.6 7.1 %fusion.93 = (f32[2,384]{1,0:T(2,128)S(1)}, f32[2,384,2304]{2,1,0:T(8,128)}) fusion(f32[384,2304]{1,0:T(8,128)} %bitcast.143, bf16[384,2,64]{0,2,1:T(8,128)(2,1)S(1)} %bitcast.150, bf16[2304,2,64]{0,2,1:T(8,128)(2,1)S(1)} %bitcast.144), kind=kOutput, calls=%fused_computation.74.clone.1 | convolution fusion | flops 233572608 | bytes 11308032 | tf_op jit(solution)/shard_map/while/body/eval_jaxpr/sub | solution.py:99
  129.7 3.8 fusion.94
  136.5 1.6 multiply_convert_fusion.2
  141.5 1.6 constant_dynamic-update-slice_fusion.17
  147.8 2.5 copy.50
  150.3 7.1 %fusion.93 = (f32[2,384]{1,0:T(2,128)S(1)}, f32[2,384,2304]{2,1,0:T(8,128)}) fusion(f32[384,2304]{1,0:T(8,128)} %bitcast.143, bf16[384,2,64]{0,2,1:T(8,128)(2,1)S(1)} %bitcast.150, bf16[2304,2,64]{0,2,1:T(8,128)(2,1)S(1)} %bitcast.144), kind=kOutput, calls=%fused_computation.74.clone.1 | convolution fusion | flops 233572608 | bytes 11308032 | tf_op jit(solution)/shard_map/while/body/eval_jaxpr/sub | solution.py:99
  157.4 3.8 fusion.94
  164.3 1.6 multiply_convert_fusion.2
  169.2 1.5 constant_dynamic-update-slice_fusion.17
  175.5 2.5 copy.50
  178.0 7.1 %fusion.93 = (f32[2,384]{1,0:T(2,128)S(1)}, f32[2,384,2304]{2,1,0:T(8,128)}) fusion(f32[384,2304]{1,0:T(8,128)} %bitcast.143, bf16[384,2,64]{0,2,1:T(8,128)(2,1)S(1)} %bitcast.150, bf16[2304,2,64]{0,2,1:T(8,128)(2,1)S(1)} %bitcast.144), kind=kOutput, calls=%fused_computation.74.clone.1 | convolution fusion | flops 233572608 | bytes 11308032 | tf_op jit(solution)/shard_map/while/body/eval_jaxpr/sub | solution.py:99
  185.1 3.8 fusion.94
  191.9 1.6 multiply_convert_fusion.2
  196.9 1.6 constant_dynamic-update-slice_fusion.17
  198.5 5.9 fusion.16
  204.4 6.2 %collective-permute-start.6 = (f32[384,1024]{0,1:T(8,128)}, f32[384,1024]{0,1:T(8,128)S(1)}, u32[]{:S(2)}, u32[]{:S(2)}) collective-permute-start(f32[384,1024]{0,1:T(8,128)} %get-tuple-element.137), channel_id=1, source_target_pairs={{1,0},{2,1},{3,2},{4,3},{5,4},{6,5},{7,6},{8,7},{9,8},{10,9},{11,1... | collective-permute-start | bytes 4718600 | tf_op jit(solution)/shard_map/ppermute | solution.py:23
  210.7 2.6 collective-permute-start.7
  213.2 4.3 collective-permute-start.9
  217.5 1.3 collective-permute-start.8
  218.9 1.4 fusion.23
  220.3 2.0 convolution_bitcast_fusion.1
  222.3 90.3 %collective-permute-done.5 = f32[384,1024]{0,1:T(8,128)S(1)} collective-permute-done((f32[384,1024]{0,1:T(8,128)}, f32[384,1024]{0,1:T(8,128)S(1)}, u32[]{:S(2)}, u32[]{:S(2)}) %collective-permute-start.5) | collective-permute-done | bytes 1572896 | tf_op jit(solution)/shard_map/ppermute | solution.py:20
  313.2 1.8 convolution_bitcast_fusion
  315.0 1.5 fusion.34
  317.7 2.7 fusion.38
  320.4 3.4 fusion.21
  323.8 264.0 %all-reduce.3.cloned.1.call-done = (f32[512,512]{0,1:T(8,128)}, f32[512,512]{0,1:T(8,128)}, f32[512,512]{0,1:T(8,128)}, f32[512,512]{1,0:T(8,128)}) async-done(((f32[512,512]{0,1:T(8,128)}, f32[512,512]{0,1:T(8,128)}, f32[512,512]{0,1:T(8,128)}, f32[512,512]{1,0:T(8,128)}), (f32[512,512]{0,1:T(8,128)}, f32[512,512]{0,1:T(8,128)}, f32[512,512]{0,1:T(8,128)}, ...) | async-done | bytes 4194320 | tf_op jit(solution)/shard_map/psum | solution.py:136
  587.9 2.7 copy.24
  590.5 2.5 copy.25
  593.1 1.3 copy.26
  (149 shorter events, 48.2 us)
Async XLA Ops:
  7.2 20.5 %copy-start = (bf16[512,512]{1,0:T(8,128)(2,1)S(1)}, bf16[512,512]{1,0:T(8,128)(2,1)}, u32[]{:S(2)}) copy-start(bf16[512,512]{1,0:T(8,128)(2,1)} %param.15) | copy-start | bytes 1572868
  7.2 20.0 %copy-start.4 = (bf16[1,384,512]{2,1,0:T(8,128)(2,1)S(1)}, bf16[1,384,512]{2,1,0:T(8,128)(2,1)}, u32[]{:S(2)}) copy-start(bf16[1,384,512]{2,1,0:T(8,128)(2,1)} %param.9) | copy-start | bytes 1179652
  7.2 20.0 %copy-start.6 = (bf16[512,512]{1,0:T(8,128)(2,1)S(1)}, bf16[512,512]{1,0:T(8,128)(2,1)}, u32[]{:S(2)}) copy-start(bf16[512,512]{1,0:T(8,128)(2,1)} %param.12) | copy-start | bytes 1572868
  7.2 20.4 %copy-start.14 = (s32[1,3,18]{2,0,1:T(1,128)S(1)}, s32[1,3,18]{2,0,1:T(1,128)}, u32[]{:S(2)}) copy-start(s32[1,3,18]{2,0,1:T(1,128)} %param.10) | copy-start | bytes 652
  7.2 20.4 %copy-start.9 = (bf16[1,384,512]{2,1,0:T(8,128)(2,1)S(1)}, bf16[1,384,512]{2,1,0:T(8,128)(2,1)}, u32[]{:S(2)}) copy-start(bf16[1,384,512]{2,1,0:T(8,128)(2,1)} %param.11) | copy-start | bytes 1179652
  7.2 580.6 %all-reduce.3.cloned.1.call-start = ((), (), s32[]{:S(2)}) async-start(), calls=%async_computation | async-start | bytes 8388608 | tf_op jit(solution)/shard_map/psum | solution.py:136
  9.6 1.0 copy-start.2
  13.3 68.6 %collective-permute-start.4 = (bf16[384,1024]{1,0:T(8,128)(2,1)}, bf16[384,1024]{1,0:T(8,128)(2,1)S(1)}, u32[]{:S(2)}, u32[]{:S(2)}) collective-permute-start(bf16[384,1024]{1,0:T(8,128)(2,1)} %get-tuple-element.146), channel_id=1, source_target_pairs={{0,16},{1,17},{2,18},{3,19},{4,20},{5,21},{6,22},{7,23},{8,24},{9,... | collective-permute-start | bytes 2359304 | tf_op jit(solution)/shard_map/ppermute | solution.py:31
  20.5 59.3 %collective-permute-start.3 = (bf16[384,1024]{1,0:T(8,128)(2,1)}, bf16[384,1024]{1,0:T(8,128)(2,1)}, u32[]{:S(2)}, u32[]{:S(2)}) collective-permute-start(bf16[384,1024]{1,0:T(8,128)(2,1)} %get-tuple-element.146), channel_id=1, source_target_pairs={{0,32},{1,33},{2,34},{3,35},{4,36},{5,37},{6,38},{7,39},{8,40},{9,... | collective-permute-start | bytes 2359304 | tf_op jit(solution)/shard_map/ppermute | solution.py:31
  21.0 56.8 %collective-permute-start.2 = (bf16[384,1024]{1,0:T(8,128)(2,1)}, bf16[384,1024]{1,0:T(8,128)(2,1)}, u32[]{:S(2)}, u32[]{:S(2)}) collective-permute-start(bf16[384,1024]{1,0:T(8,128)(2,1)} %get-tuple-element.146), channel_id=1, source_target_pairs={{0,64},{1,65},{2,66},{3,67},{4,68},{5,69},{6,70},{7,71},{8,72},{9,... | collective-permute-start | bytes 2359304 | tf_op jit(solution)/shard_map/ppermute | solution.py:31
  23.6 52.1 %collective-permute-start.1 = (bf16[384,1024]{1,0:T(8,128)(2,1)}, bf16[384,1024]{1,0:T(8,128)(2,1)}, u32[]{:S(2)}, u32[]{:S(2)}) collective-permute-start(bf16[384,1024]{1,0:T(8,128)(2,1)} %get-tuple-element.146), channel_id=1, source_target_pairs={{1,0},{2,1},{3,2},{4,3},{5,4},{6,5},{7,6},{8,7},{9,8},{10,9},{11,1... | collective-permute-start | bytes 2359304 | tf_op jit(solution)/shard_map/ppermute | solution.py:23
  27.2 46.4 %collective-permute-start = (bf16[384,1024]{1,0:T(8,128)(2,1)}, bf16[384,1024]{1,0:T(8,128)(2,1)}, u32[]{:S(2)}, u32[]{:S(2)}) collective-permute-start(bf16[384,1024]{1,0:T(8,128)(2,1)} %get-tuple-element.146), channel_id=1, source_target_pairs={{0,1},{1,2},{2,3},{3,4},{4,5},{5,6},{6,7},{7,8},{8,9},{9,10},{10,1... | collective-permute-start | bytes 2359304 | tf_op jit(solution)/shard_map/ppermute | solution.py:20
  87.6 1.5 copy-start.7
  105.8 3.0 copy-start.1
  112.4 3.0 copy-start.8
  115.4 1.5 copy-start.7
  133.5 3.0 copy-start.1
  140.1 3.0 copy-start.8
  143.1 1.5 copy-start.7
  161.3 3.0 copy-start.1
  167.8 2.9 copy-start.8
  170.8 1.5 copy-start.7
  188.9 3.0 copy-start.1
  195.5 2.9 copy-start.8
  198.4 114.2 %slice-start = ((s8[4718592]{0:T(1024)(128)(4,1)}), s8[4194304]{0:T(1024)(128)(4,1)S(1)}, s32[]{:S(2)}) async-start(s8[4718592]{0:T(1024)(128)(4,1)} %bitcast.156), calls=%async_computation.1 | async-start | bytes 8388608
  198.4 114.2 %slice-start.2 = ((s8[4718592]{0:T(1024)(128)(4,1)}), s8[4194304]{0:T(1024)(128)(4,1)S(1)}, s32[]{:S(2)}) async-start(s8[4718592]{0:T(1024)(128)(4,1)} %bitcast.160), calls=%async_computation.3 | async-start | bytes 8388608
  198.4 20.5 %copy-start.10 = (bf16[1,384,512]{2,1,0:T(8,128)(2,1)S(1)}, bf16[1,384,512]{2,1,0:T(8,128)(2,1)}, u32[]{:S(2)}) copy-start(bf16[1,384,512]{2,1,0:T(8,128)(2,1)} %param.11) | copy-start | bytes 1179652
  198.4 20.5 %copy-start.11 = (bf16[4,384,128]{1,2,0:T(8,128)(2,1)S(1)}, bf16[4,384,128]{1,2,0:T(8,128)(2,1)}, u32[]{:S(2)}) copy-start(bf16[4,384,128]{1,2,0:T(8,128)(2,1)} %get-tuple-element.66) | copy-start | bytes 1179652
  198.4 21.9 %copy-start.5 = (f32[4,384,128]{1,2,0:T(8,128)S(1)}, f32[4,384,128]{1,2,0:T(8,128)}, u32[]{:S(2)}) copy-start(f32[4,384,128]{1,2,0:T(8,128)} %get-tuple-element.67) | copy-start | bytes 2359300
  198.5 114.2 %slice-start.1 = ((s8[4718592]{0:T(1024)(128)(4,1)}), s8[524288]{0:T(1024)(128)(4,1)S(1)}, s32[]{:S(2)}) async-start(s8[4718592]{0:T(1024)(128)(4,1)} %bitcast.156), calls=%async_computation.2 | async-start | bytes 1048576
  198.5 114.2 %slice-start.3 = ((s8[4718592]{0:T(1024)(128)(4,1)}), s8[524288]{0:T(1024)(128)(4,1)S(1)}, s32[]{:S(2)}) async-start(s8[4718592]{0:T(1024)(128)(4,1)} %bitcast.160), calls=%async_computation.4 | async-start | bytes 1048576
  204.4 108.2 %collective-permute-start.5 = (f32[384,1024]{0,1:T(8,128)}, f32[384,1024]{0,1:T(8,128)S(1)}, u32[]{:S(2)}, u32[]{:S(2)}) collective-permute-start(f32[384,1024]{0,1:T(8,128)} %get-tuple-element.136), channel_id=1, source_target_pairs={{0,1},{1,2},{2,3},{3,4},{4,5},{5,6},{6,7},{7,8},{8,9},{9,10},{10,1... | collective-permute-start | bytes 4718600 | tf_op jit(solution)/shard_map/ppermute | solution.py:20
  204.4 108.2 %collective-permute-start.6 = (f32[384,1024]{0,1:T(8,128)}, f32[384,1024]{0,1:T(8,128)S(1)}, u32[]{:S(2)}, u32[]{:S(2)}) collective-permute-start(f32[384,1024]{0,1:T(8,128)} %get-tuple-element.137), channel_id=1, source_target_pairs={{1,0},{2,1},{3,2},{4,3},{5,4},{6,5},{7,6},{8,7},{9,8},{10,9},{11,1... | collective-permute-start | bytes 4718600 | tf_op jit(solution)/shard_map/ppermute | solution.py:23
  210.7 102.0 %collective-permute-start.7 = (f32[384,1024]{0,1:T(8,128)}, f32[384,1024]{0,1:T(8,128)S(1)}, u32[]{:S(2)}, u32[]{:S(2)}) collective-permute-start(f32[384,1024]{0,1:T(8,128)} %get-tuple-element.138), channel_id=1, source_target_pairs={{0,64},{1,65},{2,66},{3,67},{4,68},{5,69},{6,70},{7,71},{8,72},{9,... | collective-permute-start | bytes 4718600 | tf_op jit(solution)/shard_map/ppermute | solution.py:31
  213.2 99.4 %collective-permute-start.9 = (f32[384,1024]{0,1:T(8,128)S(1)}, f32[384,1024]{0,1:T(8,128)S(1)}, u32[]{:S(2)}, u32[]{:S(2)}) collective-permute-start(f32[384,1024]{0,1:T(8,128)S(1)} %get-tuple-element.139), channel_id=1, source_target_pairs={{0,16},{1,17},{2,18},{3,19},{4,20},{5,21},{6,22},{7,23},{8,24},{9,... | collective-permute-start | bytes 4718600 | tf_op jit(solution)/shard_map/ppermute | solution.py:31
  217.5 95.1 %collective-permute-start.8 = (f32[384,1024]{0,1:T(8,128)S(1)}, f32[384,1024]{0,1:T(8,128)S(1)}, u32[]{:S(2)}, u32[]{:S(2)}) collective-permute-start(f32[384,1024]{0,1:T(8,128)S(1)} %get-tuple-element.140), channel_id=1, source_target_pairs={{0,32},{1,33},{2,34},{3,35},{4,36},{5,37},{6,38},{7,39},{8,40},{9,... | collective-permute-start | bytes 4718600 | tf_op jit(solution)/shard_map/ppermute | solution.py:31
  316.5 3.9 copy-start.3
  587.9 5.2 copy-start.13
  587.9 6.5 %copy-start.12 = (f32[512,512]{1,0:T(8,128)S(1)}, f32[512,512]{1,0:T(8,128)}, u32[]{:S(2)}) copy-start(f32[512,512]{1,0:T(8,128)} %get-tuple-element.276) | copy-start | bytes 3145732
Sparse Core Ops, SparseCore 0:
  316.7 271.1 all-reduce.2
where the time goes:
time: 603 us; the launch traced here: 602 us
  waiting for transfers between devices  400 us (66%)
  local copies, waits for them, and re-layouts  68.6 us (11%)
  matrix products  66.2 us (11%)
  starting transfers between devices  28.4 us (5%)
  other arithmetic  21.8 us (4%)
  between operations  14.3 us (2%)
    psum x1, waiting for transfers between devices, per_device(): lax.psum((g_query, g_both[:, :width_all], g_both[:, width_all:], g_out),...  264 us
    ppermute x2, waiting for transfers between devices, with_halo(): lax.ppermute(lax.slice_in_dim(block, block.shape[dim] - width, None, axis...  136 us
    sub x4, matrix products, head_pair(): exp_vals = jnp.exp(scores - row_max)  28.3 us
    ppermute x6, starting transfers between devices, from_partner(): return lax.ppermute(value, axis, pairs)  18.5 us
    unnamed x41, local copies, waits for them, and re-layouts  18.1 us
    convert_element_type x4, other arithmetic, head_pair(): prob_bf = prob_f32.astype(jnp.bfloat16)  15.3 us
    while x28, local copies, waits for them, and re-layouts  14.3 us
  transfers between devices with their start and end apart: 11, of which 3 were waited for; matrix products, arithmetic and copies ran while one was open for 3% of the time, Pallas kernels for 0%

commit v1 on v0

--- a/solution.py
+++ b/solution.py
@@ -9,6 +9,14 @@
 TILE_DEV = 3
 NB = 3
 CANDT = 18
+
+
+def plan_the_stops_all(here_x):
+    row_axis = "dp"
+    mesh_ax = "dom"
+    for p in (mesh_ax, row_axis):
+        here_x = lax.psum(here_x, axis_name=p)
+    return here_x
 
 
 def with_halo(block, sides, width):
@@ -133,8 +141,8 @@
     grad_x = jnp.dot(grad_q, w_query.astype(jnp.float32).T, precision=highest) + kv_dx
     g_query = jnp.dot(rows_f32.T, grad_q, precision=highest)
     g_out = jnp.dot(out_rows.T, cot_rows, preferred_element_type=jnp.float32)
-    g_query, g_key, g_value, g_out = lax.psum(
-        (g_query, g_both[:, :width_all], g_both[:, width_all:], g_out), ("dp", "dom")
+    g_query, g_key, g_value, g_out = plan_the_stops_all(
+        (g_query, g_both[:, :width_all], g_both[:, width_all:], g_out)
     )
     return (attended[None], grad_x.astype(jnp.bfloat16)[None], g_query, g_key, g_value, g_out)
 

time: 603 us -> 611 us (1.013)
    psum x1 -> x2, waiting for transfers between devices: 264 us -> 270 us  [plan_the_stops_all(): here_x = lax.psum(here_x, axis_name=p)]
  transfers between devices with their start and end apart: 11 -> 12, of which waited for: 3 -> 4; matrix products, arithmetic and copies ran while one was open for 3% -> 3% of each run, Pallas kernels for 0% -> 0%
where the time goes in v1:
time: 611 us; the launch traced here: 608 us
  waiting for transfers between devices  406 us (66%)
  local copies, waits for them, and re-layouts  68.5 us (11%)
  matrix products  66.3 us (11%)
  starting transfers between devices  28.4 us (5%)
  other arithmetic  21.8 us (4%)
  between operations  14.3 us (2%)
    psum x2, waiting for transfers between devices, plan_the_stops_all(): here_x = lax.psum(here_x, axis_name=p)  270 us
    ppermute x2, waiting for transfers between devices, with_halo(): lax.ppermute(lax.slice_in_dim(block, block.shape[dim] - width, None, axis...  136 us
    sub x4, matrix products, head_pair(): exp_vals = jnp.exp(scores - row_max)  28.4 us
    ppermute x6, starting transfers between devices, from_partner(): return lax.ppermute(value, axis, pairs)  18.5 us
    unnamed x41, local copies, waits for them, and re-layouts  18 us
    convert_element_type x4, other arithmetic, head_pair(): prob_bf = prob_f32.astype(jnp.bfloat16)  15.3 us
    while x28, local copies, waits for them, and re-layouts  14.3 us
  transfers between devices with their start and end apart: 12, of which 4 were waited for; matrix products, arithmetic and copies ran while one was open for 3% of the time, Pallas kernels for 0%

profile of v1, /device:TPU:8, one launch (start us, length us, event | category | flops | bytes accessed | tf_op | source)
XLA Modules:
  0.0 608.3 jit_solution(467972987141503662)
XLA Ops:
  10.6 2.7 constant_dynamic-update-slice_fusion.11
  13.3 7.2 %collective-permute-start.4 = (bf16[384,1024]{1,0:T(8,128)(2,1)}, bf16[384,1024]{1,0:T(8,128)(2,1)S(1)}, u32[]{:S(2)}, u32[]{:S(2)}) collective-permute-start(bf16[384,1024]{1,0:T(8,128)(2,1)} %get-tuple-element.150), channel_id=1, source_target_pairs={{0,16},{1,17},{2,18},{3,19},{4,20},{5,21},{6,22},{7,23},{8,24},{9,... | collective-permute-start | bytes 2359304 | tf_op jit(solution)/shard_map/ppermute | solution.py:39
  21.0 2.6 collective-permute-start.2
  23.5 3.6 collective-permute-start.1
  28.1 45.5 %collective-permute-done = bf16[384,1024]{1,0:T(8,128)(2,1)} collective-permute-done((bf16[384,1024]{1,0:T(8,128)(2,1)}, bf16[384,1024]{1,0:T(8,128)(2,1)}, u32[]{:S(2)}, u32[]{:S(2)}) %collective-permute-start) | collective-permute-done | bytes 786464 | tf_op jit(solution)/shard_map/ppermute | solution.py:28
  73.5 2.1 constant_dynamic-update-slice_fusion.10
  75.6 2.1 constant_dynamic-update-slice_fusion.9
  77.7 2.1 constant_dynamic-update-slice_fusion.8
  79.8 2.1 constant_dynamic-update-slice_fusion.7
  82.8 4.8 fusion.33
  87.6 110.8 %while.16 = (s32[]{:T(128)}, bf16[4,384,128]{1,2,0:T(8,128)(2,1)}, f32[4,384,128]{1,2,0:T(8,128)}, f32[4,2304,128]{1,2,0:T(8,128)}, f32[4,2304,128]{1,2,0:T(8,12...) while((s32[]{:T(128)}, bf16[4,384,128]{1,2,0:T(8,128)(2,1)}, ...), condition=%wide.region_3.4_spmd, body=%wide.region_0.3_spmd.sunk | while | flops 1378665984 | bytes 104414744 | solution.py:129
  92.3 2.5 copy.50
  94.8 7.1 %fusion.93 = (f32[2,384]{1,0:T(2,128)S(1)}, f32[2,384,2304]{2,1,0:T(8,128)}) fusion(f32[384,2304]{1,0:T(8,128)} %bitcast.143, bf16[384,2,64]{0,2,1:T(8,128)(2,1)S(1)} %bitcast.150, bf16[2304,2,64]{0,2,1:T(8,128)(2,1)S(1)} %bitcast.144), kind=kOutput, calls=%fused_computation.74.clone.1 | convolution fusion | flops 233572608 | bytes 11308032 | tf_op jit(solution)/shard_map/while/body/eval_jaxpr/sub | solution.py:107
  101.9 3.8 fusion.94
  108.7 1.6 multiply_convert_fusion.2
  113.7 1.7 constant_dynamic-update-slice_fusion.17
  120.1 2.5 copy.50
  122.6 7.1 %fusion.93 = (f32[2,384]{1,0:T(2,128)S(1)}, f32[2,384,2304]{2,1,0:T(8,128)}) fusion(f32[384,2304]{1,0:T(8,128)} %bitcast.143, bf16[384,2,64]{0,2,1:T(8,128)(2,1)S(1)} %bitcast.150, bf16[2304,2,64]{0,2,1:T(8,128)(2,1)S(1)} %bitcast.144), kind=kOutput, calls=%fused_computation.74.clone.1 | convolution fusion | flops 233572608 | bytes 11308032 | tf_op jit(solution)/shard_map/while/body/eval_jaxpr/sub | solution.py:107
  129.7 3.8 fusion.94
  136.5 1.6 multiply_convert_fusion.2
  141.5 1.6 constant_dynamic-update-slice_fusion.17
  147.8 2.5 copy.50
  150.3 7.1 %fusion.93 = (f32[2,384]{1,0:T(2,128)S(1)}, f32[2,384,2304]{2,1,0:T(8,128)}) fusion(f32[384,2304]{1,0:T(8,128)} %bitcast.143, bf16[384,2,64]{0,2,1:T(8,128)(2,1)S(1)} %bitcast.150, bf16[2304,2,64]{0,2,1:T(8,128)(2,1)S(1)} %bitcast.144), kind=kOutput, calls=%fused_computation.74.clone.1 | convolution fusion | flops 233572608 | bytes 11308032 | tf_op jit(solution)/shard_map/while/body/eval_jaxpr/sub | solution.py:107
  157.4 3.8 fusion.94
  164.3 1.6 multiply_convert_fusion.2
  169.2 1.6 constant_dynamic-update-slice_fusion.17
  175.5 2.5 copy.50
  178.0 7.1 %fusion.93 = (f32[2,384]{1,0:T(2,128)S(1)}, f32[2,384,2304]{2,1,0:T(8,128)}) fusion(f32[384,2304]{1,0:T(8,128)} %bitcast.143, bf16[384,2,64]{0,2,1:T(8,128)(2,1)S(1)} %bitcast.150, bf16[2304,2,64]{0,2,1:T(8,128)(2,1)S(1)} %bitcast.144), kind=kOutput, calls=%fused_computation.74.clone.1 | convolution fusion | flops 233572608 | bytes 11308032 | tf_op jit(solution)/shard_map/while/body/eval_jaxpr/sub | solution.py:107
  185.1 3.8 fusion.94
  191.9 1.6 multiply_convert_fusion.2
  196.9 1.5 constant_dynamic-update-slice_fusion.17
  198.5 5.9 fusion.16
  204.4 6.2 %collective-permute-start.6 = (f32[384,1024]{0,1:T(8,128)}, f32[384,1024]{0,1:T(8,128)S(1)}, u32[]{:S(2)}, u32[]{:S(2)}) collective-permute-start(f32[384,1024]{0,1:T(8,128)} %get-tuple-element.141), channel_id=1, source_target_pairs={{1,0},{2,1},{3,2},{4,3},{5,4},{6,5},{7,6},{8,7},{9,8},{10,9},{11,1... | collective-permute-start | bytes 4718600 | tf_op jit(solution)/shard_map/ppermute | solution.py:31
  210.6 2.6 collective-permute-start.7
  213.2 4.3 collective-permute-start.9
  217.6 1.3 collective-permute-start.8
  218.9 1.5 fusion.23
  220.4 2.0 convolution_bitcast_fusion.1
  222.3 90.3 %collective-permute-done.5 = f32[384,1024]{0,1:T(8,128)S(1)} collective-permute-done((f32[384,1024]{0,1:T(8,128)}, f32[384,1024]{0,1:T(8,128)S(1)}, u32[]{:S(2)}, u32[]{:S(2)}) %collective-permute-start.5) | collective-permute-done | bytes 1572896 | tf_op jit(solution)/shard_map/ppermute | solution.py:28
  313.2 1.8 convolution_bitcast_fusion
  315.1 1.5 fusion.34
  316.6 236.8 %all-reduce.5.cloned.1.call-done = (f32[512,512]{0,1:T(8,128)}, f32[512,512]{0,1:T(8,128)}, f32[512,512]{0,1:T(8,128)}, f32[512,512]{1,0:T(8,128)}) async-done(((f32[512,512]{0,1:T(8,128)}, f32[512,512]{0,1:T(8,128)}, f32[512,512]{0,1:T(8,128)}, f32[512,512]{1,0:T(8,128)}), (f32[512,512]{0,1:T(8,128)}, f32[512,512]{0,1:T(8,128)}, f32[512,512]{0,1:T(8,128)}, ...) | async-done | bytes 4194320 | tf_op jit(solution)/shard_map/psum | solution.py:18
  554.6 2.7 fusion.38
  557.3 3.4 fusion.21
  560.7 33.2 %all-reduce.7.cloned.1.call-done = (f32[512,512]{0,1:T(8,128)}, f32[512,512]{0,1:T(8,128)}, f32[512,512]{0,1:T(8,128)}, f32[512,512]{1,0:T(8,128)}) async-done(((f32[512,512]{0,1:T(8,128)}, f32[512,512]{0,1:T(8,128)}, f32[512,512]{0,1:T(8,128)}, f32[512,512]{1,0:T(8,128)}), (f32[512,512]{0,1:T(8,128)}, f32[512,512]{0,1:T(8,128)}, f32[512,512]{0,1:T(8,128)}, ...) | async-done | bytes 4194320 | tf_op jit(solution)/shard_map/psum | solution.py:18
  593.9 2.7 copy.24
  596.6 2.5 copy.25
  599.1 1.3 copy.26
  (152 shorter events, 49.4 us)
Async XLA Ops:
  7.2 20.5 %copy-start = (bf16[512,512]{1,0:T(8,128)(2,1)S(1)}, bf16[512,512]{1,0:T(8,128)(2,1)}, u32[]{:S(2)}) copy-start(bf16[512,512]{1,0:T(8,128)(2,1)} %param.15) | copy-start | bytes 1572868
  7.2 20.0 %copy-start.4 = (bf16[1,384,512]{2,1,0:T(8,128)(2,1)S(1)}, bf16[1,384,512]{2,1,0:T(8,128)(2,1)}, u32[]{:S(2)}) copy-start(bf16[1,384,512]{2,1,0:T(8,128)(2,1)} %param.9) | copy-start | bytes 1179652
  7.2 20.0 %copy-start.6 = (bf16[512,512]{1,0:T(8,128)(2,1)S(1)}, bf16[512,512]{1,0:T(8,128)(2,1)}, u32[]{:S(2)}) copy-start(bf16[512,512]{1,0:T(8,128)(2,1)} %param.12) | copy-start | bytes 1572868
  7.2 20.4 %copy-start.14 = (s32[1,3,18]{2,0,1:T(1,128)S(1)}, s32[1,3,18]{2,0,1:T(1,128)}, u32[]{:S(2)}) copy-start(s32[1,3,18]{2,0,1:T(1,128)} %param.10) | copy-start | bytes 652
  7.2 20.4 %copy-start.9 = (bf16[1,384,512]{2,1,0:T(8,128)(2,1)S(1)}, bf16[1,384,512]{2,1,0:T(8,128)(2,1)}, u32[]{:S(2)}) copy-start(bf16[1,384,512]{2,1,0:T(8,128)(2,1)} %param.11) | copy-start | bytes 1179652
  7.2 546.2 %all-reduce.5.cloned.1.call-start = ((), (), s32[]{:S(2)}) async-start(), calls=%async_computation | async-start | bytes 8388608 | tf_op jit(solution)/shard_map/psum | solution.py:18
  9.6 1.0 copy-start.2
  13.3 68.5 %collective-permute-start.4 = (bf16[384,1024]{1,0:T(8,128)(2,1)}, bf16[384,1024]{1,0:T(8,128)(2,1)S(1)}, u32[]{:S(2)}, u32[]{:S(2)}) collective-permute-start(bf16[384,1024]{1,0:T(8,128)(2,1)} %get-tuple-element.150), channel_id=1, source_target_pairs={{0,16},{1,17},{2,18},{3,19},{4,20},{5,21},{6,22},{7,23},{8,24},{9,... | collective-permute-start | bytes 2359304 | tf_op jit(solution)/shard_map/ppermute | solution.py:39
  20.5 59.3 %collective-permute-start.3 = (bf16[384,1024]{1,0:T(8,128)(2,1)}, bf16[384,1024]{1,0:T(8,128)(2,1)}, u32[]{:S(2)}, u32[]{:S(2)}) collective-permute-start(bf16[384,1024]{1,0:T(8,128)(2,1)} %get-tuple-element.150), channel_id=1, source_target_pairs={{0,32},{1,33},{2,34},{3,35},{4,36},{5,37},{6,38},{7,39},{8,40},{9,... | collective-permute-start | bytes 2359304 | tf_op jit(solution)/shard_map/ppermute | solution.py:39
  21.0 56.7 %collective-permute-start.2 = (bf16[384,1024]{1,0:T(8,128)(2,1)}, bf16[384,1024]{1,0:T(8,128)(2,1)}, u32[]{:S(2)}, u32[]{:S(2)}) collective-permute-start(bf16[384,1024]{1,0:T(8,128)(2,1)} %get-tuple-element.150), channel_id=1, source_target_pairs={{0,64},{1,65},{2,66},{3,67},{4,68},{5,69},{6,70},{7,71},{8,72},{9,... | collective-permute-start | bytes 2359304 | tf_op jit(solution)/shard_map/ppermute | solution.py:39
  23.5 52.1 %collective-permute-start.1 = (bf16[384,1024]{1,0:T(8,128)(2,1)}, bf16[384,1024]{1,0:T(8,128)(2,1)}, u32[]{:S(2)}, u32[]{:S(2)}) collective-permute-start(bf16[384,1024]{1,0:T(8,128)(2,1)} %get-tuple-element.150), channel_id=1, source_target_pairs={{1,0},{2,1},{3,2},{4,3},{5,4},{6,5},{7,6},{8,7},{9,8},{10,9},{11,1... | collective-permute-start | bytes 2359304 | tf_op jit(solution)/shard_map/ppermute | solution.py:31
  27.2 46.4 %collective-permute-start = (bf16[384,1024]{1,0:T(8,128)(2,1)}, bf16[384,1024]{1,0:T(8,128)(2,1)}, u32[]{:S(2)}, u32[]{:S(2)}) collective-permute-start(bf16[384,1024]{1,0:T(8,128)(2,1)} %get-tuple-element.150), channel_id=1, source_target_pairs={{0,1},{1,2},{2,3},{3,4},{4,5},{5,6},{6,7},{7,8},{8,9},{9,10},{10,1... | collective-permute-start | bytes 2359304 | tf_op jit(solution)/shard_map/ppermute | solution.py:28
  87.6 1.5 copy-start.7
  105.7 3.0 copy-start.1
  112.3 3.0 copy-start.8
  115.3 1.5 copy-start.7
  133.5 3.0 copy-start.1
  140.1 3.0 copy-start.8
  143.1 1.5 copy-start.7
  161.2 3.0 copy-start.1
  167.8 2.9 copy-start.8
  170.8 1.5 copy-start.7
  188.9 3.0 copy-start.1
  195.5 2.9 copy-start.8
  198.4 114.3 %slice-start = ((s8[4718592]{0:T(1024)(128)(4,1)}), s8[4194304]{0:T(1024)(128)(4,1)S(1)}, s32[]{:S(2)}) async-start(s8[4718592]{0:T(1024)(128)(4,1)} %bitcast.156), calls=%async_computation.2 | async-start | bytes 8388608
  198.4 114.3 %slice-start.2 = ((s8[4718592]{0:T(1024)(128)(4,1)}), s8[4194304]{0:T(1024)(128)(4,1)S(1)}, s32[]{:S(2)}) async-start(s8[4718592]{0:T(1024)(128)(4,1)} %bitcast.160), calls=%async_computation.4 | async-start | bytes 8388608
  198.4 20.5 %copy-start.10 = (bf16[1,384,512]{2,1,0:T(8,128)(2,1)S(1)}, bf16[1,384,512]{2,1,0:T(8,128)(2,1)}, u32[]{:S(2)}) copy-start(bf16[1,384,512]{2,1,0:T(8,128)(2,1)} %param.11) | copy-start | bytes 1179652
  198.4 20.5 %copy-start.11 = (bf16[4,384,128]{1,2,0:T(8,128)(2,1)S(1)}, bf16[4,384,128]{1,2,0:T(8,128)(2,1)}, u32[]{:S(2)}) copy-start(bf16[4,384,128]{1,2,0:T(8,128)(2,1)} %get-tuple-element.66) | copy-start | bytes 1179652
  198.4 21.9 %copy-start.5 = (f32[4,384,128]{1,2,0:T(8,128)S(1)}, f32[4,384,128]{1,2,0:T(8,128)}, u32[]{:S(2)}) copy-start(f32[4,384,128]{1,2,0:T(8,128)} %get-tuple-element.67) | copy-start | bytes 2359300
  198.4 114.2 %slice-start.1 = ((s8[4718592]{0:T(1024)(128)(4,1)}), s8[524288]{0:T(1024)(128)(4,1)S(1)}, s32[]{:S(2)}) async-start(s8[4718592]{0:T(1024)(128)(4,1)} %bitcast.156), calls=%async_computation.3 | async-start | bytes 1048576
  198.4 114.2 %slice-start.3 = ((s8[4718592]{0:T(1024)(128)(4,1)}), s8[524288]{0:T(1024)(128)(4,1)S(1)}, s32[]{:S(2)}) async-start(s8[4718592]{0:T(1024)(128)(4,1)} %bitcast.160), calls=%async_computation.5 | async-start | bytes 1048576
  204.4 108.2 %collective-permute-start.5 = (f32[384,1024]{0,1:T(8,128)}, f32[384,1024]{0,1:T(8,128)S(1)}, u32[]{:S(2)}, u32[]{:S(2)}) collective-permute-start(f32[384,1024]{0,1:T(8,128)} %get-tuple-element.140), channel_id=1, source_target_pairs={{0,1},{1,2},{2,3},{3,4},{4,5},{5,6},{6,7},{7,8},{8,9},{9,10},{10,1... | collective-permute-start | bytes 4718600 | tf_op jit(solution)/shard_map/ppermute | solution.py:28
  204.4 108.2 %collective-permute-start.6 = (f32[384,1024]{0,1:T(8,128)}, f32[384,1024]{0,1:T(8,128)S(1)}, u32[]{:S(2)}, u32[]{:S(2)}) collective-permute-start(f32[384,1024]{0,1:T(8,128)} %get-tuple-element.141), channel_id=1, source_target_pairs={{1,0},{2,1},{3,2},{4,3},{5,4},{6,5},{7,6},{8,7},{9,8},{10,9},{11,1... | collective-permute-start | bytes 4718600 | tf_op jit(solution)/shard_map/ppermute | solution.py:31
  210.6 102.0 %collective-permute-start.7 = (f32[384,1024]{0,1:T(8,128)}, f32[384,1024]{0,1:T(8,128)S(1)}, u32[]{:S(2)}, u32[]{:S(2)}) collective-permute-start(f32[384,1024]{0,1:T(8,128)} %get-tuple-element.142), channel_id=1, source_target_pairs={{0,64},{1,65},{2,66},{3,67},{4,68},{5,69},{6,70},{7,71},{8,72},{9,... | collective-permute-start | bytes 4718600 | tf_op jit(solution)/shard_map/ppermute | solution.py:39
  213.2 99.4 %collective-permute-start.9 = (f32[384,1024]{0,1:T(8,128)S(1)}, f32[384,1024]{0,1:T(8,128)S(1)}, u32[]{:S(2)}, u32[]{:S(2)}) collective-permute-start(f32[384,1024]{0,1:T(8,128)S(1)} %get-tuple-element.143), channel_id=1, source_target_pairs={{0,16},{1,17},{2,18},{3,19},{4,20},{5,21},{6,22},{7,23},{8,24},{9,... | collective-permute-start | bytes 4718600 | tf_op jit(solution)/shard_map/ppermute | solution.py:39
  217.6 95.1 %collective-permute-start.8 = (f32[384,1024]{0,1:T(8,128)S(1)}, f32[384,1024]{0,1:T(8,128)S(1)}, u32[]{:S(2)}, u32[]{:S(2)}) collective-permute-start(f32[384,1024]{0,1:T(8,128)S(1)} %get-tuple-element.144), channel_id=1, source_target_pairs={{0,32},{1,33},{2,34},{3,35},{4,36},{5,37},{6,38},{7,39},{8,40},{9,... | collective-permute-start | bytes 4718600 | tf_op jit(solution)/shard_map/ppermute | solution.py:39
  316.6 277.4 %all-reduce.7.cloned.1.call-start = ((), (), s32[]{:S(2)}) async-start(), calls=%async_computation.1 | async-start | bytes 8388608 | tf_op jit(solution)/shard_map/psum | solution.py:18
  553.4 3.9 copy-start.3
  593.9 5.2 copy-start.13
  593.9 6.5 %copy-start.12 = (f32[512,512]{1,0:T(8,128)S(1)}, f32[512,512]{1,0:T(8,128)}, u32[]{:S(2)}) copy-start(f32[512,512]{1,0:T(8,128)} %get-tuple-element.280) | copy-start | bytes 3145732
Sparse Core Ops, SparseCore 0:
  316.7 236.6 all-reduce.4
  556.7 37.1 all-reduce.6
